TPU v7x, 128 devices: a whole 4x4x4 slice. The times are simulated.
128 devices in a mesh: rep: 8 (over y, x_lo), row: 16 (over x_hi, z, core).
Axes of the slice: x: 4 (x_hi: 2, x_lo: 2; x = x_hi * 2 + x_lo), y: 4, z: 4, core: 2. Of those that a mesh axis runs over, the one named last changes fastest.
Arguments:
- features: bfloat16 [262144, 128], P(('rep', 'row')), may hold values from -6 to 6
- degrees: int32 [262144], P(('rep', 'row')), may hold values from 4 to 128
- tile_values: bfloat16 [98304, 128, 128], P(('rep', 'row')), may hold values from 0 to 3, as said below
- tile_rows: int32 [98304], P(('rep', 'row')), may hold values from 0 to 127
- tile_cols: int32 [98304], P(('rep', 'row')), may hold values from 0 to 255
- tile_live: int32 [128], P(('rep', 'row')), may hold values from 384 to 768, as said below
- weight: bfloat16 [128, 128], replicated, may hold values from -0.5 to 0.5
- bias: float32 [128], replicated, may hold values from -1 to 1
Outputs:
- activations: bfloat16 [262144, 128], P(('rep', 'row'))
Inputs may be any that keep to these rules, and one draw needn't show every extreme that they name: `tile_live`: at least one device has all 768 slots live. `tile_values`: sparse tiles of small integer edge counts, mostly zeros and ones.
All inputs are finite; a program needn't handle non-finite values.
Results may differ from a plain program's by a relative error of at most 0.0053.
Values may be sent and summed in bfloat16 or wider, within the bound.
A program may use at most 256 MiB of HBM per device.

v0:
```python
import jax
import jax.numpy as jnp
from jax import lax
from jax.sharding import PartitionSpec as P


def per_device(features, degrees, tile_values, tile_rows, tile_cols, tile_live, weight, bias):
    owned = features.shape[0]
    per_block = owned // 128
    groups = lax.axis_size("rep")
    slots_here = tile_values.shape[0]
    width = features.shape[1]
    scale = lax.rsqrt(degrees.astype(jnp.float32))
    scaled = (features.astype(jnp.float32) * scale[:, None]).astype(jnp.bfloat16)
    gathered = lax.all_gather(scaled, "row", axis=0, tiled=True)
    col_tiles = gathered.reshape(-1, 128, width)[tile_cols]
    prods = jnp.einsum("kab,kbf->kaf", tile_values, col_tiles, preferred_element_type=jnp.float32)
    alive = (jnp.arange(slots_here, dtype=jnp.int32) < tile_live[0]).astype(jnp.float32)
    prods = prods * alive[:, None, None]
    partial_value = jax.ops.segment_sum(prods, tile_rows, num_segments=groups * per_block)
    partial_value = partial_value.reshape(groups * owned, width)
    totals = lax.psum(partial_value, "rep")
    own_sum = lax.dynamic_slice_in_dim(totals, lax.axis_index("rep") * owned, owned, 0)
    aggregated = (own_sum * scale[:, None]).astype(jnp.bfloat16)
    mixed = jnp.dot(aggregated, weight, preferred_element_type=jnp.float32) + bias[None, :]
    return jax.nn.relu(mixed).astype(jnp.bfloat16)


def solution(mesh):
    return jax.shard_map(
        per_device,
        mesh=mesh,
        in_specs=(
            P(("rep", "row"), None),
            P(("rep", "row")),
            P(("rep", "row"), None, None),
            P(("rep", "row")),
            P(("rep", "row")),
            P(("rep", "row")),
            P(),
            P(),
        ),
        out_specs=P(("rep", "row"), None),
        check_vma=False,
    )
```

profile of v0, /device:TPU:1, one launch (start us, length us, event | category | flops | bytes accessed | tf_op | source)
XLA Modules:
  0.0 703.8 jit_solution(4155334828526962372)
XLA Ops:
  6.5 0.0 copy-start
  6.5 0.0 all-gather.2.cloned.1.call-start
  6.5 0.7 convert_rsqrt_fusion
  7.3 2.2 multiply_convert_fusion.1
  9.4 0.0 all-gather.2.cloned.1.call-update
  9.5 0.0 all-reduce.2.cloned.1.call-start
  10.1 0.7 compare_select_fusion
  10.9 75.8 %all-gather.2.cloned.1.call-done = bf16[32768,128]{1,0:T(8,128)(2,1)} async-done(((bf16[2048,128]{1,0:T(8,128)(2,1)}), bf16[32768,128]{1,0:T(8,128)(2,1)}) %all-gather.2.cloned.1.call-update) | async-done | bytes 8388624 | tf_op jit(solution)/shard_map/all_gather | solution.py:15
  86.6 22.6 %gather_fusion = bf16[768,128,128]{2,1,0:T(8,128)(2,1)} fusion(bf16[256,128,128]{2,1,0:T(8,128)(2,1)} %bitcast.10, s32[1024]{0:T(1024)S(1)} %pad_clamp_fusion), kind=kCustom, calls=%fused_computation | custom fusion | bytes 50334720 | tf_op jit(solution)/shard_map/gather | solution.py:16
  109.2 40.7 %multiply_bitcast_fusion = f32[768,128,128]{1,2,0:T(8,128)} fusion(f32[768]{0:T(1024)S(1)} %fusion.3, bf16[768,128,128]{2,1,0:T(8,128)(2,1)} %gather_fusion, bf16[768,128,128]{2,1,0:T(8,128)(2,1)} %param.10), kind=kOutput, calls=%fused_computation.2 | convolution fusion | flops 3233808384 | bytes 100666368 | tf_op jit(solution)/shard_map/kab,kbf->kaf/dot_general | solution.py:17
  149.9 0.0 copy-start.1
  149.9 48.8 %copy.11 = f32[768,128,128]{2,1,0:T(8,128)} copy(f32[768,128,128]{1,2,0:T(8,128)} %multiply_bitcast_fusion) | data formatting | bytes 100663296 | tf_op jit(solution)/shard_map/mul | solution.py:19
  198.7 4.3 broadcast_in_dim.6
  203.0 0.0 copy-done.1
  203.0 0.0 copy-start.2
  203.0 154.5 %scatter_fusion = f32[128,128,128]{2,1,0:T(8,128)} fusion(f32[128,128,128]{2,1,0:T(8,128)} %broadcast_in_dim.6, s32[768]{0:T(1024)S(1)} %copy-done.1, f32[768,128,128]{2,1,0:T(8,128)} %copy.11), kind=kCustom, calls=%fused_computation.1 | custom fusion | flops 12582912 | bytes 150998016 | tf_op jit(solution)/shard_map/scatter-add | solution.py:20
  357.5 0.0 all-reduce.2.cloned.1.call-update
  357.5 337.0 %all-reduce.2.cloned.1.call-done = f32[16384,128]{1,0:T(8,128)} async-done(((f32[16384,128]{1,0:T(8,128)}), f32[16384,128]{1,0:T(8,128)}) %all-reduce.2.cloned.1.call-update) | async-done | bytes 8388624 | tf_op jit(solution)/shard_map/psum | solution.py:22
  694.5 0.0 copy-done
  694.5 0.0 copy-done.2
  694.5 2.5 fusion.1
  (2 shorter events, 0.0 us)
Async XLA Ops:
  6.5 687.9 %copy-start = (bf16[128,128]{1,0:T(8,128)(2,1)S(1)}, bf16[128,128]{1,0:T(8,128)(2,1)}, u32[]{:S(2)}) copy-start(bf16[128,128]{1,0:T(8,128)(2,1)} %param.14) | copy-start | bytes 98308
  6.5 80.1 %all-gather.2.cloned.1.call-start = ((), (), s32[]{:S(2)}) async-start(), calls=%async_computation | async-start | bytes 8912896 | tf_op jit(solution)/shard_map/all_gather | solution.py:15
  9.5 685.0 %all-reduce.2.cloned.1.call-start = ((), (), s32[]{:S(2)}) async-start(), calls=%async_computation.1 | async-start | bytes 16777216 | tf_op jit(solution)/shard_map/psum | solution.py:22
  149.9 53.1 %copy-start.1 = (s32[768]{0:T(1024)S(1)}, s32[768]{0:T(1024)}, u32[]{:S(2)}) copy-start(s32[768]{0:T(1024)} %param.11) | copy-start | bytes 9220
  203.0 491.5 %copy-start.2 = (f32[128]{0:T(128)S(1)}, f32[128]{0:T(128)}, u32[]{:S(2)}) copy-start(f32[128]{0:T(128)} %param.15) | copy-start | bytes 1540
Sparse Core Ops, SparseCore 0:
  9.8 76.7 all-gather.1
  357.6 336.7 all-reduce.1
where the time goes:
time: 706 us; the launch traced here: 704 us
  waiting for transfers between devices  413 us (58%)
  other arithmetic  158 us (22%)
  local copies, waits for them, and re-layouts  75.7 us (11%)
  matrix products  43.2 us (6%)
  between operations  14.1 us (2%)
    psum x1, waiting for transfers between devices, per_device(): totals = lax.psum(partial_value, 'rep')  337 us
    scatter-add x1, other arithmetic, per_device(): jax.ops.segment_sum(prods, tile_rows, num_segments=groups * per_block)  154 us
    all_gather x1, waiting for transfers between devices, per_device(): gathered = lax.all_gather(scaled, 'row', axis=0, tiled=True)  75.8 us
    mul x1, local copies, waits for them, and re-layouts, per_device(): prods = prods * alive[:, None, None]  48.8 us
    dot_general x1, matrix products, per_device(): jnp.einsum('kab,kbf->kaf', tile_values, col_tiles, preferred_element_type...  40.7 us
    gather x1, local copies, waits for them, and re-layouts, per_device(): col_tiles = gathered.reshape(-1, 128, width)[tile_cols]  22.6 us
  transfers between devices with their start and end apart: 2, of which 2 were waited for; matrix products, arithmetic and copies ran while one was open for 0% of the time, Pallas kernels for 0%

commit v1 on v0

--- a/solution.py
+++ b/solution.py
@@ -12,7 +12,9 @@
     width = features.shape[1]
     scale = lax.rsqrt(degrees.astype(jnp.float32))
     scaled = (features.astype(jnp.float32) * scale[:, None]).astype(jnp.bfloat16)
-    gathered = lax.all_gather(scaled, "row", axis=0, tiled=True)
+    gathered = jnp.concatenate(
+        lax.all_to_all(jnp.stack([scaled] * lax.axis_size("row")), "row", 0, 0), axis=0
+    )
     col_tiles = gathered.reshape(-1, 128, width)[tile_cols]
     prods = jnp.einsum("kab,kbf->kaf", tile_values, col_tiles, preferred_element_type=jnp.float32)
     alive = (jnp.arange(slots_here, dtype=jnp.int32) < tile_live[0]).astype(jnp.float32)

time: 706 us -> 773 us (1.095)
  waiting for transfers between devices: 413 us -> 467 us
  starting transfers between devices: 0.04 us -> 9.33 us
    all_to_all x0 -> x1, waiting for transfers between devices: none -> 119 us  [per_device(): lax.all_to_all(jnp.stack([scaled] * lax.axis_size('row')), 'row', 0, 0)]
    all_gather x1 -> x0, waiting for transfers between devices: 75.8 us -> none  [per_device(): gathered = lax.all_gather(scaled, 'row', axis=0, tiled=True)]
    psum x1, waiting for transfers between devices: 337 us -> 348 us  [per_device(): totals = lax.psum(partial_value, 'rep')]
    all_to_all x0 -> x1, starting transfers between devices: none -> 9.29 us  [per_device(): lax.all_to_all(jnp.stack([scaled] * lax.axis_size('row')), 'row', 0, 0)]
where the time goes in v1:
time: 773 us; the launch traced here: 771 us
  waiting for transfers between devices  467 us (60%)
  other arithmetic  157 us (20%)
  local copies, waits for them, and re-layouts  80.5 us (10%)
  matrix products  43.2 us (6%)
  between operations  14.1 us (2%)
  starting transfers between devices  9.33 us (1%)
    psum x1, waiting for transfers between devices, per_device(): totals = lax.psum(partial_value, 'rep')  348 us
    scatter-add x1, other arithmetic, per_device(): jax.ops.segment_sum(prods, tile_rows, num_segments=groups * per_block)  154 us
    all_to_all x1, waiting for transfers between devices, per_device(): lax.all_to_all(jnp.stack([scaled] * lax.axis_size('row')), 'row', 0, 0)  119 us
    mul x1, local copies, waits for them, and re-layouts, per_device(): prods = prods * alive[:, None, None]  48.8 us
    dot_general x1, matrix products, per_device(): jnp.einsum('kab,kbf->kaf', tile_values, col_tiles, preferred_element_type...  40.7 us
    gather x1, local copies, waits for them, and re-layouts, per_device(): col_tiles = gathered.reshape(-1, 128, width)[tile_cols]  22.6 us
  transfers between devices with their start and end apart: 2, of which 2 were waited for; matrix products, arithmetic and copies ran while one was open for 0% of the time, Pallas kernels for 0%

profile of v1, /device:TPU:1, one launch (start us, length us, event | category | flops | bytes accessed | tf_op | source)
XLA Modules:
  0.0 770.8 jit_solution(16568189540638337659)
XLA Ops:
  6.5 0.0 copy-start
  6.5 0.0 copy-start.2
  6.5 0.7 convert_rsqrt_fusion
  7.3 1.4 multiply_convert_fusion.1
  8.6 4.8 stack.2
  13.5 9.3 %all-to-all-start = ((bf16[16,2048,128]{2,1,0:T(8,128)(2,1)}), bf16[16,2048,128]{2,1,0:T(8,128)(2,1)}, u32[]{:S(2)}, u32[]{:S(2)}) async-start(bf16[16,2048,128]{2,1,0:T(8,128)(2,1)} %stack.2), calls=%async_computation | async-start | bytes 16777216 | tf_op jit(solution)/shard_map/all_to_all | solution.py:16
  22.8 0.0 all-reduce.2.cloned.1.call-start
  23.5 0.0 copy-done.2
  23.5 118.7 %all-to-all-done = bf16[16,2048,128]{2,1,0:T(8,128)(2,1)} async-done(((bf16[16,2048,128]{2,1,0:T(8,128)(2,1)}), bf16[16,2048,128]{2,1,0:T(8,128)(2,1)}, u32[]{:S(2)}, u32[]{:S(2)}) %all-to-all-start) | async-done | bytes 8388640 | tf_op jit(solution)/shard_map/all_to_all | solution.py:16
  142.2 22.6 %gather_fusion = bf16[768,128,128]{2,1,0:T(8,128)(2,1)} fusion(bf16[256,128,128]{2,1,0:T(8,128)(2,1)} %bitcast, s32[1024]{0:T(1024)S(1)} %pad_clamp_fusion), kind=kCustom, calls=%fused_computation | custom fusion | bytes 50334720 | tf_op jit(solution)/shard_map/gather | solution.py:18
  164.8 40.7 %multiply_bitcast_fusion = f32[768,128,128]{1,2,0:T(8,128)} fusion(f32[768]{0:T(1024)S(1)} %fusion.3, bf16[768,128,128]{2,1,0:T(8,128)(2,1)} %gather_fusion, bf16[768,128,128]{2,1,0:T(8,128)(2,1)} %param.10), kind=kOutput, calls=%fused_computation.2 | convolution fusion | flops 3233808384 | bytes 100666368 | tf_op jit(solution)/shard_map/kab,kbf->kaf/dot_general | solution.py:19
  205.5 0.0 copy-start.1
  205.5 48.8 %copy.11 = f32[768,128,128]{2,1,0:T(8,128)} copy(f32[768,128,128]{1,2,0:T(8,128)} %multiply_bitcast_fusion) | data formatting | bytes 100663296 | tf_op jit(solution)/shard_map/mul | solution.py:21
  254.3 4.3 broadcast_in_dim.6
  258.6 0.0 copy-done.1
  258.6 0.0 copy-start.3
  258.6 154.5 %scatter_fusion = f32[128,128,128]{2,1,0:T(8,128)} fusion(f32[128,128,128]{2,1,0:T(8,128)} %broadcast_in_dim.6, s32[768]{0:T(1024)S(1)} %copy-done.1, f32[768,128,128]{2,1,0:T(8,128)} %copy.11), kind=kCustom, calls=%fused_computation.1 | custom fusion | flops 12582912 | bytes 150998016 | tf_op jit(solution)/shard_map/scatter-add | solution.py:22
  413.0 0.0 all-reduce.2.cloned.1.call-update
  413.1 348.4 %all-reduce.2.cloned.1.call-done = f32[16384,128]{1,0:T(8,128)} async-done(((f32[16384,128]{1,0:T(8,128)}), f32[16384,128]{1,0:T(8,128)}) %all-reduce.2.cloned.1.call-update) | async-done | bytes 8388624 | tf_op jit(solution)/shard_map/psum | solution.py:24
  761.5 0.0 copy-done
  761.5 0.0 copy-done.3
  761.5 2.5 fusion.1
  (3 shorter events, 0.0 us)
Async XLA Ops:
  6.5 755.0 %copy-start = (bf16[128,128]{1,0:T(8,128)(2,1)S(1)}, bf16[128,128]{1,0:T(8,128)(2,1)}, u32[]{:S(2)}) copy-start(bf16[128,128]{1,0:T(8,128)(2,1)} %param.14) | copy-start | bytes 98308
  6.5 16.9 %copy-start.2 = (s32[768]{0:T(1024)S(1)}, s32[768]{0:T(1024)}, u32[]{:S(2)}) copy-start(s32[768]{0:T(1024)} %param.12) | copy-start | bytes 9220
  13.5 128.7 %all-to-all-start = ((bf16[16,2048,128]{2,1,0:T(8,128)(2,1)}), bf16[16,2048,128]{2,1,0:T(8,128)(2,1)}, u32[]{:S(2)}, u32[]{:S(2)}) async-start(bf16[16,2048,128]{2,1,0:T(8,128)(2,1)} %stack.2), calls=%async_computation | async-start | bytes 16777216 | tf_op jit(solution)/shard_map/all_to_all | solution.py:16
  22.8 738.7 %all-reduce.2.cloned.1.call-start = ((), (), s32[]{:S(2)}) async-start(), calls=%async_computation.1 | async-start | bytes 16777216 | tf_op jit(solution)/shard_map/psum | solution.py:24
  205.5 53.1 %copy-start.1 = (s32[768]{0:T(1024)S(1)}, s32[768]{0:T(1024)}, u32[]{:S(2)}) copy-start(s32[768]{0:T(1024)} %param.11) | copy-start | bytes 9220
  258.6 502.9 %copy-start.3 = (f32[128]{0:T(128)S(1)}, f32[128]{0:T(128)}, u32[]{:S(2)}) copy-start(f32[128]{0:T(128)} %param.15) | copy-start | bytes 1540
Sparse Core Ops, SparseCore 0:
  413.2 348.2 all-reduce.1
